TPU v7x, 512 devices: a whole 4x8x8 slice. The times are simulated.
512 devices in a mesh: group: 64 (over x, y, core), tensor: 8 (over z).
Axes of the slice: x: 4, y: 8, z: 8, core: 2. Of those that a mesh axis runs over, the one named last changes fastest.
Arguments:
- tokens: bfloat16 [24576, 8192], P('group', 'tensor'), may hold values from -6 to 6
- w_key: bfloat16 [8192, 1024], P('tensor'), may hold values from -0.0625 to 0.0625
- row_adapter: int32 [24576, 1], P('group'), may hold values from 0 to 127; in each aligned block of 384 rows (0 to 383, 384 to 767, ...) at most 4 rows name the same one
- panel_a: bfloat16 [128, 8192, 64], P('group', 'tensor'), may hold values from -0.0625 to 0.0625
- up_panels: bfloat16 [128, 64, 1024], P('group'), may hold values from -0.75 to 0.75
Outputs:
- keys: bfloat16 [1024, 24576], P('tensor', 'group')
Inputs may be any that keep to these rules, and one draw needn't show every extreme that they name: `row_adapter`: in the rows of one group (aligned blocks of 384 rows) no adapter is named by more than 4 rows; in every draw some group names some adapter exactly 4 times.
All inputs are finite; a program needn't handle non-finite values.
Results may differ from a plain program's by a relative error of at most 0.0095.
Values may be sent and summed in bfloat16 or wider, within the bound.
A program may use at most 64 MiB of HBM per device.

v0:
```python
import jax
import jax.numpy as jnp
from jax import lax
from jax.sharding import PartitionSpec as P


def local(tokens, w_key, row_adapter, panel_a, up_panels):
    group_count = lax.axis_size("group")
    row_count = tokens.shape[0]
    local_width = tokens.shape[1]
    adapter_number = panel_a.shape[0] * group_count
    slot_capacity = max(2, 3 * row_count // (2 * adapter_number))
    adapter_ids = row_adapter[:, 0]
    one_hot = (adapter_ids[:, None] == jnp.arange(adapter_number, dtype=jnp.int32)[None, :]).astype(
        jnp.bfloat16
    )
    row_iota = lax.broadcasted_iota(jnp.int32, (row_count, row_count), 0)
    col_iota = lax.broadcasted_iota(jnp.int32, (row_count, row_count), 1)
    earlier = (col_iota < row_iota).astype(jnp.bfloat16)
    before = jnp.dot(earlier, one_hot, preferred_element_type=jnp.float32)
    slot_rank = jnp.sum(before * one_hot.astype(jnp.float32), axis=1).astype(jnp.int32)
    slot_position_index = adapter_ids * slot_capacity + slot_rank
    slot_rows = jnp.full((adapter_number * slot_capacity,), row_count, jnp.int32)
    slot_rows = slot_rows.at[slot_position_index].set(jnp.arange(row_count, dtype=jnp.int32))
    padded = jnp.concatenate([tokens, jnp.zeros((1, local_width), tokens.dtype)], axis=0)
    outgoing = padded[slot_rows].reshape(adapter_number, slot_capacity, local_width)
    incoming = lax.all_to_all(outgoing, "group", split_axis=0, concat_axis=1, tiled=True)
    partial_rank = jnp.einsum("asd,adr->asr", incoming, panel_a, preferred_element_type=jnp.float32)
    widened_rows = jnp.einsum(
        "asr,ark->ask", partial_rank, up_panels.astype(jnp.float32), precision=lax.Precision.HIGHEST
    )
    gathered_back = lax.all_to_all(
        widened_rows.astype(jnp.bfloat16), "group", split_axis=1, concat_axis=0, tiled=True
    ).astype(widened_rows.dtype)
    row_lowrank = gathered_back.reshape(adapter_number * slot_capacity, widened_rows.shape[2])[
        slot_position_index
    ]
    summed = lax.psum_scatter(
        lax.dot_general(w_key, tokens, (((0,), (1,)), ((), ())), preferred_element_type=jnp.float32)
        + row_lowrank.T,
        "tensor",
        scatter_dimension=0,
        tiled=True,
    )
    return summed.astype(jnp.bfloat16)


def solution(mesh):
    return jax.shard_map(
        local,
        mesh=mesh,
        in_specs=(
            P("group", "tensor"),
            P("tensor", None),
            P("group", None),
            P("group", "tensor", None),
            P("group", None, None),
        ),
        out_specs=P("tensor", "group"),
        check_vma=False,
    )
```

profile of v0, /device:TPU:6, one launch (start us, length us, event | category | flops | bytes accessed | tf_op | source)
XLA Modules:
  0.0 164.7 jit_solution(10230105210707860142)
XLA Ops:
  6.5 0.0 copy-start
  6.5 0.8 reduce
  7.4 0.2 fusion
  7.6 0.7 fusion.5
  8.4 2.9 %scatter_custom_fusion = s32[512]{0:T(512)S(1)} fusion(s32[384]{0:T(512)S(1)} %fusion.5, s32[384]{0:T(512)S(1)} %iota.19, s32[]{:T(128)} %constant.0.clone.1), kind=kCustom, calls=%fused_computation.19 | custom fusion | bytes 2052 | tf_op jit(solution)/shard_map/scatter | solution.py:24
  11.3 1.2 concatenate.3
  12.5 2.8 %gather_fusion = bf16[512,1024]{1,0:T(8,128)(2,1)} fusion(bf16[385,1024]{1,0:T(8,128)(2,1)S(1)} %concatenate.3, s32[1024]{0:T(1024)S(1)} %pad_clamp_fusion.1), kind=kCustom, calls=%fused_computation | custom fusion | bytes 2099200 | tf_op jit(solution)/shard_map/gather | solution.py:26
  15.3 1.5 reshape.17
  16.8 37.3 %all_to_all.27 = bf16[128,4,1024]{2,1,0:T(4,128)(2,1)S(1)} all-to-all(bf16[128,4,1024]{2,1,0:T(4,128)(2,1)S(1)} %reshape.17), channel_id=1, replica_groups=mesh['group'=64,'tensor'=8] {'group'}, dimensions={0} | all-to-all | bytes 2097152 | tf_op jit(solution)/shard_map/all_to_all | solution.py:27
  54.0 0.0 copy-start.3
  54.0 0.0 copy-start.2
  54.0 1.1 copy.14
  55.1 0.0 copy-done.3
  55.1 0.4 fusion.1
  55.5 0.0 copy-done.2
  55.6 1.0 convolution_convert_fusion
  56.6 2.1 %copy.16 = bf16[2,256,1024]{2,0,1:T(2,128)(2,1)} copy(bf16[2,256,1024]{2,1,0:T(8,128)(2,1)S(1)} %convolution_convert_fusion) | data formatting | bytes 2097152 | tf_op jit(solution)/shard_map/convert_element_type | solution.py:33
  58.7 8.1 %all-to-all-start.1 = ((bf16[2,256,1024]{2,0,1:T(2,128)(2,1)}), bf16[2,256,1024]{2,0,1:T(2,128)(2,1)S(1)}, u32[]{:S(2)}, u32[]{:S(2)}) async-start(bf16[2,256,1024]{2,0,1:T(2,128)(2,1)} %copy.16), calls=%async_computation.1 | async-start | bytes 2097152 | tf_op jit(solution)/shard_map/all_to_all | solution.py:32
  66.8 0.0 reduce-scatter.2.cloned.1.call-start
  66.8 26.6 %all-to-all-done.1 = bf16[2,256,1024]{2,0,1:T(2,128)(2,1)S(1)} async-done(((bf16[2,256,1024]{2,0,1:T(2,128)(2,1)}), bf16[2,256,1024]{2,0,1:T(2,128)(2,1)S(1)}, u32[]{:S(2)}, u32[]{:S(2)}) %all-to-all-start.1) | async-done | bytes 1048608 | tf_op jit(solution)/shard_map/all_to_all | solution.py:32
  93.4 1.9 %copy.22 = f32[2,64,4,1024]{3,2,0,1:T(4,128)} copy(bf16[2,64,4,1024]{3,0,2,1:T(2,128)(2,1)S(1)} %bitcast.17) | data formatting | bytes 3145728 | tf_op jit(solution)/shard_map/convert_element_type | solution.py:34
  95.3 3.0 %reshape.18 = f32[512,1024]{1,0:T(8,128)} reshape(f32[64,2,4,1024]{3,2,1,0:T(4,128)} %bitcast.16) | data formatting | bytes 4194304 | tf_op jit(solution)/shard_map/convert_element_type | solution.py:34
  98.3 5.0 %gather_fusion.1 = f32[384,1024]{1,0:T(8,128)} fusion(f32[512,1024]{1,0:T(8,128)} %reshape.18, s32[1024]{0:T(1024)S(1)} %pad_clamp_fusion), kind=kCustom, calls=%fused_computation.1 | custom fusion | bytes 3147264 | tf_op jit(solution)/shard_map/gather | solution.py:35
  103.3 0.0 copy-start.1
  103.4 3.1 %copy.18 = f32[384,1024]{0,1:T(8,128)} copy(f32[384,1024]{1,0:T(8,128)} %gather_fusion.1) | data formatting | bytes 3145728 | tf_op jit(solution)/shard_map/gather | solution.py:35
  106.5 0.0 copy-done
  106.5 0.0 copy-done.1
  106.5 3.9 %bitcast_add_fusion = f32[1024,384]{1,0:T(8,128)} fusion(f32[384,1024]{0,1:T(8,128)} %copy.18, bf16[1024,1024]{1,0:T(8,128)(2,1)S(1)} %copy-done, bf16[384,1024]{1,0:T(8,128)(2,1)S(1)} %copy-done.1), kind=kOutput, calls=%fused_computation.4 | convolution fusion | flops 805699584 | bytes 6029312 | tf_op jit(solution)/shard_map/dot_general | solution.py:39
  110.3 0.0 reduce-scatter.2.cloned.1.call-update
  110.4 45.9 %reduce-scatter.2.cloned.1.call-done = f32[128,384]{1,0:T(8,128)} async-done(((f32[1024,384]{1,0:T(8,128)}), f32[128,384]{1,0:T(8,128)}) %reduce-scatter.2.cloned.1.call-update) | async-done | bytes 196624 | tf_op jit(solution)/shard_map/reduce_scatter | solution.py:38
  156.2 1.6 convert_element_type.49
  (5 shorter events, 0.0 us)
Async XLA Ops:
  6.5 99.9 %copy-start = (bf16[1024,1024]{1,0:T(8,128)(2,1)S(1)}, bf16[1024,1024]{1,0:T(8,128)(2,1)}, u32[]{:S(2)}) copy-start(bf16[1024,1024]{1,0:T(8,128)(2,1)} %param.6) | copy-start | bytes 6291460
  54.0 1.1 copy-start.3
  54.0 1.5 copy-start.2
  58.7 34.8 %all-to-all-start.1 = ((bf16[2,256,1024]{2,0,1:T(2,128)(2,1)}), bf16[2,256,1024]{2,0,1:T(2,128)(2,1)S(1)}, u32[]{:S(2)}, u32[]{:S(2)}) async-start(bf16[2,256,1024]{2,0,1:T(2,128)(2,1)} %copy.16), calls=%async_computation.1 | async-start | bytes 2097152 | tf_op jit(solution)/shard_map/all_to_all | solution.py:32
  66.8 89.5 %reduce-scatter.2.cloned.1.call-start = ((), (), s32[]{:S(2)}) async-start(), calls=%async_computation.3 | async-start | bytes 1769472 | tf_op jit(solution)/shard_map/reduce_scatter | solution.py:38
  103.3 3.1 %copy-start.1 = (bf16[384,1024]{1,0:T(8,128)(2,1)S(1)}, bf16[384,1024]{1,0:T(8,128)(2,1)}, u32[]{:S(2)}) copy-start(bf16[384,1024]{1,0:T(8,128)(2,1)} %param.5) | copy-start | bytes 2359300
Sparse Core Ops, SparseCore 0:
  110.5 45.7 reduce-scatter.1
where the time goes:
time: 165 us
  waiting for transfers between devices  72.5 us (44%)
  blocking collectives  37.3 us (23%)
  local copies, waits for them, and re-layouts  24.6 us (15%)
  between operations  13.5 us (8%)
  starting transfers between devices  8.14 us (5%)
  matrix products  5.57 us (3%)
  other arithmetic  3.15 us (2%)
    reduce_scatter x1, waiting for transfers between devices, local(): lax.psum_scatter(lax.dot_general(w_key, tokens, (((0,), (1,)), ((), ())),...  45.9 us
    all_to_all x1, blocking collectives, local(): lax.all_to_all(outgoing, 'group', split_axis=0, concat_axis=1, tiled=True)  37.3 us
    all_to_all x1, waiting for transfers between devices, local(): lax.all_to_all(widened_rows.astype(jnp.bfloat16), 'group', split_axis=1,...  26.6 us
    gather x2, local copies, waits for them, and re-layouts, local(): gathered_back.reshape(adapter_number * slot_capacity, widened_rows.shape[2])  8.12 us
    all_to_all x1, starting transfers between devices, local(): lax.all_to_all(widened_rows.astype(jnp.bfloat16), 'group', split_axis=1,...  8.1 us
    convert_element_type x2, local copies, waits for them, and re-layouts, local(): gathered_back = lax.all_to_all(widened_rows.astype(jnp.bfloat16), 'group'...  4.92 us
    dot_general x1, matrix products, local(): lax.dot_general(w_key, tokens, (((0,), (1,)), ((), ())), preferred_elemen...  3.86 us
  transfers between devices with their start and end apart: 2, of which 2 were waited for; matrix products, arithmetic and copies ran while one was open for 0% of the time, Pallas kernels for 0%

commit v1 on v0

v1 whole, which is shorter than its diff:
```python
import functools

import jax
import jax.numpy as jnp
from jax import lax
from jax.experimental import pallas as pl
from jax.experimental.pallas import tpu as pltpu
from jax.sharding import PartitionSpec as P

MESH = pl.DeviceIdType.MESH
F32, BF16 = jnp.float32, jnp.bfloat16
X, Y = 4, 8
CAP = 4


def kernel(dims, ids_ref, tok_hbm, w_hbm, pa_hbm, up_hbm, out_ref,
           tok, w, pa, up, place, send, recv, bsend, brecv, base, rsend, rrecv, lsend, lrecv,
           in_sem, tok_ss, tok_rs, b_ss, b_rs, r_ss, r_rs, l_ss, l_rs):
    nx, ny, nz = dims
    nxc = 2 * nx
    ng = nxc * ny
    sets = ng // nz
    rows, width = tok.shape
    half = width // 2
    feat, keys = out_ref.shape[0], w.shape[1]
    slots = 2 * CAP
    self_at = ((nxc - ny % nxc) % nxc) * ny + ny - 1

    me, t = lax.axis_index("group"), lax.axis_index("tensor")
    mc, my, mx = lax.rem(me, 2), lax.rem(lax.div(me, 2), ny), lax.div(me, 2 * ny)

    def offsets(i):
        k, m = lax.div(i, ny), lax.rem(i, ny)
        h = lax.div(m, 2)
        odd = lax.rem(m, 2)
        dy = odd * (ny // 2 - 1 - h) + (1 - odd) * (ny // 2 + h)
        q = lax.rem(k + m + 1, nxc)
        return lax.div(q, 2), dy, lax.rem(q, 2)

    def dest(i):
        dx, dy, dc = offsets(i)
        return (lax.rem(mx + dx, nx) * ny + lax.rem(my + dy, ny)) * 2 + lax.rem(mc + dc, 2)

    def source(i):
        dx, dy, dc = offsets(i)
        return (lax.rem(mx - dx + nx, nx) * ny + lax.rem(my - dy + ny, ny)) * 2 + lax.rem(mc + dc, 2)

    loads = [pltpu.make_async_copy(a, b, in_sem.at[n])
             for n, (a, b) in enumerate(((tok_hbm, tok), (w_hbm, w), (pa_hbm, pa), (up_hbm, up)))]
    for c in loads:
        c.start()

    barrier = pltpu.get_barrier_semaphore()

    @pl.loop(0, ng)
    def _(i):
        @pl.when(i != self_at)
        def _():
            pl.semaphore_signal(barrier, inc=1, device_id={"group": dest(i)}, device_id_type=MESH)

    @pl.loop(1, nz)
    def _(j):
        pl.semaphore_signal(barrier, inc=1, device_id={"tensor": lax.rem(t + j, nz)}, device_id_type=MESH)

    ids = ids_ref[...]
    one_hot = (lax.broadcasted_iota(jnp.int32, (2 * ng, rows), 0) == ids).astype(F32)
    earlier = (lax.broadcasted_iota(jnp.int32, (rows, rows), 0)
               < lax.broadcasted_iota(jnp.int32, (rows, rows), 1)).astype(F32).astype(BF16)
    before = jnp.dot(one_hot.astype(BF16), earlier, preferred_element_type=F32)
    rank = jnp.sum(before * one_hot, axis=0, keepdims=True)
    slot = ids.astype(F32) * CAP + rank
    total = ng * slots
    part = min(128, total)
    loads[0].wait()
    for c in range(total // part):
        at = lax.broadcasted_iota(jnp.int32, (part, rows), 0).astype(F32) + float(c * part)
        chosen = (at == slot).astype(F32).astype(BF16)
        place[c * part:(c + 1) * part, :] = chosen
        g = jnp.dot(chosen, tok[...], preferred_element_type=F32)
        n = part // slots
        both = jnp.concatenate([g[:, :half].reshape(n, slots, half), g[:, half:].reshape(n, slots, half)], axis=1)
        send[c * n:(c + 1) * n] = both.astype(BF16)

    pl.semaphore_wait(barrier, ng - 1 + nz - 1)

    def token_copy(i, n=1):
        d = dest(i)
        return pltpu.make_async_remote_copy(
            send.at[d], recv.at[i], tok_ss, tok_rs.at[i], device_id={"group": d}, device_id_type=MESH)

    @pl.loop(0, ng)
    def _(i):
        @pl.when(i != self_at)
        def _():
            token_copy(i).start()

    recv[self_at] = send[me]

    def base_part(peer):
        block = w[:, pl.ds(pl.multiple_of(peer * feat, feat), feat)]
        return lax.dot_general(block, tok[...], (((0,), (1,)), ((), ())), preferred_element_type=F32)

    def base_copy(j):
        return pltpu.make_async_remote_copy(
            bsend.at[j], brecv.at[j], b_ss.at[j], b_rs.at[j],
            device_id={"tensor": lax.rem(t + j, nz)}, device_id_type=MESH)

    loads[1].wait()

    @pl.loop(0, nz - 1)
    def _(n):
        h, odd = lax.div(n, 2), lax.rem(n, 2)
        j = odd * (nz // 2 - 1 - h) + (1 - odd) * (nz // 2 + h)
        bsend[j] = base_part(lax.rem(t + j, nz)).astype(BF16)
        base_copy(j).start()

    base[...] = base_part(t)

    loads[2].wait()
    loads[3].wait()
    panel = jnp.concatenate([pa[0, :, :half], pa[1, :, :half], pa[0, :, half:], pa[1, :, half:]], axis=0)
    rk = pa.shape[1]
    ups = jnp.concatenate([up[0], up[1], up[0], up[1]], axis=0)

    def rank_copy(k):
        return pltpu.make_async_remote_copy(
            rsend.at[k], rrecv.at[t], r_ss.at[k], r_rs.at[t], device_id={"tensor": k}, device_id_type=MESH)

    def rank_from(p):
        return pltpu.make_async_remote_copy(
            rsend.at[p], rrecv.at[p], r_ss.at[p], r_rs.at[p], device_id={"tensor": p}, device_id_type=MESH)

    def swap(v):
        return jnp.concatenate([v[:, CAP:], v[:, :CAP]], axis=1)

    pair_shape = (sets // 2, slots, 2 * rk)
    top = lax.broadcasted_iota(jnp.int32, pair_shape, 1) < CAP
    first = lax.broadcasted_iota(jnp.int32, pair_shape, 2) < rk

    def lora_copy(n):
        s, p = lax.div(n, nz), lax.rem(n, nz)
        return pltpu.make_async_remote_copy(
            lsend.at[s, p], lrecv.at[me], l_ss.at[n], l_rs.at[me],
            device_id={"group": source(t * sets + s), "tensor": p}, device_id_type=MESH)

    def lora_stays(n):
        return (t * sets + lax.div(n, nz) == self_at) & (lax.rem(n, nz) == t)

    @pl.loop(0, nz + 1)
    def _(k):
        @pl.when(k < nz)
        def _():
            @pl.loop(0, sets)
            def _(s):
                i = k * sets + s

                @pl.when(i != self_at)
                def _():
                    token_copy(i).wait_recv()

            x = recv[pl.ds(k * sets, sets)].reshape(sets * 2 * slots, half)
            r = lax.dot_general(x, panel, (((1,), (1,)), ((), ())), preferred_element_type=F32)
            r = r.reshape(sets, 2 * slots, 4 * rk)
            v = (r[:, :slots, :2 * rk] + r[:, slots:, 2 * rk:]).reshape(sets // 2, 2, slots, 2 * rk)
            even, odd = v[:, 0], v[:, 1]
            packed = jnp.where(top, jnp.where(first, even, swap(even)), jnp.where(first, swap(odd), odd))

            @pl.when(k != t)
            def _():
                rsend[k] = packed
                rank_copy(k).start()

            @pl.when(k == t)
            def _():
                rrecv[k] = packed

        @pl.when(k == t + 1)
        def _():
            @pl.loop(1, nz)
            def _(j):
                rank_from(lax.rem(t + j, nz)).wait_recv()

            v = rrecv[0]
            for p in range(1, nz):
                v = v + rrecv[p]
            zero = jnp.zeros_like(v)
            other = swap(v)
            even = jnp.where(top, jnp.where(first, v, zero), jnp.where(first, zero, other))
            odd = jnp.where(top, jnp.where(first, other, zero), jnp.where(first, zero, v))
            lhs = jnp.concatenate([even[:, None], odd[:, None]], axis=1).reshape(sets * slots, 2 * rk)
            high = lhs.astype(BF16)
            low = (lhs - high.astype(F32)).astype(BF16)
            lora = jnp.dot(jnp.concatenate([high, low], axis=1), ups, preferred_element_type=F32)
            for p in range(nz):
                lsend[:, p] = lora[:, p * feat:(p + 1) * feat].reshape(sets, slots, feat).astype(BF16)

            @pl.loop(0, sets * nz)
            def _(n):
                @pl.when(jnp.logical_not(lora_stays(n)))
                def _():
                    lora_copy(n).start()

            @pl.when(t == self_at // sets)
            def _():
                lrecv[me] = lsend[self_at % sets, t]

    @pl.loop(1, nz)
    def _(j):
        base_copy(j).wait_recv()

    acc = base[...]
    for j in range(1, nz):
        acc = acc + brecv[j].astype(F32)

    @pl.loop(0, ng)
    def _(g):
        @pl.when(jnp.logical_not((g == me) & (t == self_at // sets)))
        def _():
            pltpu.make_async_remote_copy(
                lsend.at[0, 0], lrecv.at[g], l_ss.at[0], l_rs.at[g],
                device_id={"group": g}, device_id_type=MESH).wait_recv()

    back = lrecv[...].astype(F32).reshape(total, feat).astype(BF16)
    acc = acc + lax.dot_general(back, place[...], (((0,), (0,)), ((), ())), preferred_element_type=F32)
    out_ref[...] = acc.astype(BF16)

    pltpu.make_async_remote_copy(
        send.at[pl.ds(0, ng - 1)], recv.at[pl.ds(0, ng - 1)], tok_ss, tok_rs.at[0],
        device_id={"group": me}, device_id_type=MESH).wait_send()

    @pl.loop(1, nz)
    def _(j):
        base_copy(j).wait_send()
        rank_copy(lax.rem(t + j, nz)).wait_send()

    @pl.loop(0, sets * nz)
    def _(n):
        @pl.when(jnp.logical_not(lora_stays(n)))
        def _():
            lora_copy(n).wait_send()


def local(dims, tokens, w_key, row_adapter, panel_a, up_panels):
    nx, ny, nz = dims
    ng = 2 * nx * ny
    rows, width = tokens.shape
    keys = w_key.shape[1]
    feat = keys // nz
    sets = ng // nz
    rk = panel_a.shape[2]
    vmem = pl.BlockSpec(memory_space=pltpu.VMEM)
    hbm = pl.BlockSpec(memory_space=pl.ANY)
    dma = pltpu.SemaphoreType.DMA
    return pl.pallas_call(
        functools.partial(kernel, dims),
        out_shape=jax.ShapeDtypeStruct((feat, rows), BF16),
        in_specs=[vmem, hbm, hbm, hbm, hbm],
        out_specs=vmem,
        scratch_shapes=[
            pltpu.VMEM((rows, width), BF16),
            pltpu.VMEM(w_key.shape, BF16),
            pltpu.VMEM((2, rk, width), BF16),
            pltpu.VMEM(up_panels.shape, BF16),
            pltpu.VMEM((2 * CAP * ng, rows), BF16),
            pltpu.VMEM((ng, 4 * CAP, width // 2), BF16),
            pltpu.VMEM((ng, 4 * CAP, width // 2), BF16),
            pltpu.VMEM((nz, feat, rows), BF16),
            pltpu.VMEM((nz, feat, rows), BF16),
            pltpu.VMEM((feat, rows), F32),
            pltpu.VMEM((nz, sets // 2, 2 * CAP, 2 * rk), F32),
            pltpu.VMEM((nz, sets // 2, 2 * CAP, 2 * rk), F32),
            pltpu.VMEM((sets, nz, 2 * CAP, feat), BF16),
            pltpu.VMEM((ng, 2 * CAP, feat), BF16),
            dma((4,)),
            dma,
            dma((ng,)),
            dma((nz,)),
            dma((nz,)),
            dma((nz,)),
            dma((nz,)),
            dma((sets * nz,)),
            dma((ng,)),
        ],
        compiler_params=pltpu.CompilerParams(
            collective_id=0, has_side_effects=True, vmem_limit_bytes=48 * 1024 * 1024),
    )(row_adapter.reshape(1, rows), tokens, w_key, jnp.swapaxes(panel_a, 1, 2), up_panels)


def solution(mesh):
    return jax.shard_map(
        functools.partial(local, (X, Y, mesh.shape["tensor"])),
        mesh=mesh,
        in_specs=(
            P("group", "tensor"),
            P("tensor", None),
            P("group", None),
            P("group", "tensor", None),
            P("group", None, None),
        ),
        out_specs=P("tensor", "group"),
        check_vma=False,
    )
```

time: 165 us -> 78.8 us (0.48)
  the two profiles are of different devices: /device:TPU:6 before, /device:TPU:1 now
where the time goes in v1:
time: 78.8 us; the launch traced here: 78.5 us
  Pallas kernels  72.5 us (92%)
  local copies, waits for them, and re-layouts  5.95 us (8%)
    pallas_call x1, Pallas kernels, local(): pl.pallas_call(functools.partial(kernel, dims), out_shape=jax.ShapeDtypeS...  72.5 us
    unnamed x11, local copies, waits for them, and re-layouts  5.95 us

profile of v1, /device:TPU:1, one launch (start us, length us, event | category | flops | bytes accessed | tf_op | source)
XLA Modules:
  0.0 78.5 jit_solution(18354079266682046323)
XLA Ops:
  0.0 0.0 copy-start
  0.0 1.6 %copy-done = bf16[1024,1024]{1,0:T(8,128)(2,1)S(1)} copy-done((bf16[1024,1024]{1,0:T(8,128)(2,1)S(1)}, bf16[1024,1024]{1,0:T(8,128)(2,1)}, u32[]{:S(2)}) %copy-start) | copy-done | bytes 2097176
  1.6 0.0 copy-start.1
  1.6 1.1 %copy-done.1 = bf16[384,1024]{1,0:T(8,128)(2,1)S(1)} copy-done((bf16[384,1024]{1,0:T(8,128)(2,1)S(1)}, bf16[384,1024]{1,0:T(8,128)(2,1)}, u32[]{:S(2)}) %copy-start.1) | copy-done | bytes 786456
  2.7 0.0 copy-start.2
  2.7 0.9 %copy-done.2 = bf16[2,1024,64]{1,2,0:T(8,128)(2,1)S(1)} copy-done((bf16[2,1024,64]{1,2,0:T(8,128)(2,1)S(1)}, bf16[2,1024,64]{1,2,0:T(8,128)(2,1)}, u32[]{:S(2)}) %copy-start.2) | copy-done | bytes 262168
  3.7 0.0 copy-start.3
  3.7 0.9 %copy-done.3 = bf16[2,64,1024]{2,1,0:T(8,128)(2,1)S(1)} copy-done((bf16[2,64,1024]{2,1,0:T(8,128)(2,1)S(1)}, bf16[2,64,1024]{2,1,0:T(8,128)(2,1)}, u32[]{:S(2)}) %copy-start.3) | copy-done | bytes 262168
  4.6 0.0 copy-start.4
  4.6 0.7 copy-done.4
  5.3 72.5 %shard_map.55 = bf16[128,384]{1,0:T(8,128)(2,1)S(1)} custom-call(s32[1,384]{1,0:T(1,128)S(1)} %bitcast.3, bf16[384,1024]{1,0:T(8,128)(2,1)S(1)} %copy-done.1, bf16[1024,1024]{1,0:T(8,128)(2,1)S(1)} %copy-done, bf16[2,64,1024]{2,1,0:T(8,128)(2,1)S(1)} %bitcast.2, bf16[2,64,1024]{2,1,0:T(8,128)(2,1)S(1)} %copy-done.3), custom_call_target="tpu_custom_call" | custom-call | tf_op jit(solution)/shard_map/pallas_call | solution.py:254
  77.9 0.6 copy.7
Async XLA Ops:
  0.0 1.6 %copy-start = (bf16[1024,1024]{1,0:T(8,128)(2,1)S(1)}, bf16[1024,1024]{1,0:T(8,128)(2,1)}, u32[]{:S(2)}) copy-start(bf16[1024,1024]{1,0:T(8,128)(2,1)} %w_hbm.1) | copy-start | bytes 6291460
  1.6 1.1 %copy-start.1 = (bf16[384,1024]{1,0:T(8,128)(2,1)S(1)}, bf16[384,1024]{1,0:T(8,128)(2,1)}, u32[]{:S(2)}) copy-start(bf16[384,1024]{1,0:T(8,128)(2,1)} %tok_hbm.1) | copy-start | bytes 2359300
  2.7 0.9 %copy-start.2 = (bf16[2,1024,64]{1,2,0:T(8,128)(2,1)S(1)}, bf16[2,1024,64]{1,2,0:T(8,128)(2,1)}, u32[]{:S(2)}) copy-start(bf16[2,1024,64]{1,2,0:T(8,128)(2,1)} %param.8) | copy-start | bytes 786436
  3.7 0.9 %copy-start.3 = (bf16[2,64,1024]{2,1,0:T(8,128)(2,1)S(1)}, bf16[2,64,1024]{2,1,0:T(8,128)(2,1)}, u32[]{:S(2)}) copy-start(bf16[2,64,1024]{2,1,0:T(8,128)(2,1)} %up_hbm.1) | copy-start | bytes 786436
  4.6 0.7 copy-start.4

commit v2 on v0

v2 whole, which is shorter than its diff:
```python
import functools

import jax
import jax.numpy as jnp
from jax import lax
from jax.experimental import pallas as pl
from jax.experimental.pallas import tpu as pltpu
from jax.sharding import PartitionSpec as P

MESH = pl.DeviceIdType.MESH
F32, BF16 = jnp.float32, jnp.bfloat16
X, Y = 4, 8
CAP = 4
BATCHES = 2


def kernel(dims, ids_ref, tok_hbm, w_hbm, pa_hbm, up_hbm, out_ref,
           tok, w, panels, place, send, recv, part, zs, zr, rsend, rrecv, full, lsend, lrecv,
           in_sem, y_ss, y_rs, x_ss, x_rs, z_ss, z_rs, r_ss, r_rs, a_ss, a_rs, l_ss, l_rs):
    nx, ny, nz = dims
    nq = 2 * nx
    half, hz = ny // 2, nz // 2
    nb = half // BATCHES
    rows, width = tok.shape
    feat = out_ref.shape[0]
    rk = panels.shape[2]
    span = nb * 4 * CAP

    me, t = lax.axis_index("group"), lax.axis_index("tensor")
    mc, my, mx = lax.rem(me, 2), lax.rem(lax.div(me, 2), ny), lax.div(me, 2 * ny)
    mq = mx * 2 + mc

    def along_x(q):
        return {"group": (lax.div(q, 2) * ny + my) * 2 + lax.rem(q, 2)}

    def along_y(step):
        return {"group": (mx * ny + lax.rem(my + step + ny, ny)) * 2 + mc}

    def along_z(p):
        return {"tensor": p}

    def remote(src, dst, ss, rs, where):
        return pltpu.make_async_remote_copy(src, dst, ss, rs, device_id=where, device_id_type=MESH)

    mine = pl.ds(pl.multiple_of(t * feat, feat), feat)
    loads = [
        pltpu.make_async_copy(pa_hbm, panels.at[0, :, :, pl.ds(0, width)], in_sem.at[0]),
        pltpu.make_async_copy(up_hbm.at[:, :, mine], panels.at[0, :, :, pl.ds(width, feat)], in_sem.at[1]),
        pltpu.make_async_copy(tok_hbm, tok, in_sem.at[2]),
        pltpu.make_async_copy(w_hbm, w, in_sem.at[3]),
    ]
    for c in loads:
        c.start()

    barrier = pltpu.get_barrier_semaphore()
    for step in (-1, 1):
        pl.semaphore_signal(barrier, inc=1, device_id=along_y(step), device_id_type=MESH)

    @pl.loop(1, nz)
    def _(j):
        pl.semaphore_signal(barrier, inc=1, device_id=along_z(lax.rem(t + j, nz)), device_id_type=MESH)

    @pl.loop(1, nq)
    def _(j):
        pl.semaphore_signal(barrier, inc=1, device_id=along_x(lax.rem(mq + j, nq)), device_id_type=MESH)

    ids = ids_ref[...]
    one_hot = (lax.broadcasted_iota(jnp.int32, (2 * nq * ny, rows), 0) == ids).astype(F32)
    earlier = (lax.broadcasted_iota(jnp.int32, (rows, rows), 0)
               < lax.broadcasted_iota(jnp.int32, (rows, rows), 1)).astype(F32).astype(BF16)
    before = jnp.dot(one_hot.astype(BF16), earlier, preferred_element_type=F32)
    rank = jnp.sum(before * one_hot, axis=0, keepdims=True)
    second, core = lax.rem(ids, 2), lax.rem(lax.div(ids, 2), 2)
    home_y, home_x = lax.rem(lax.div(ids, 4), ny), lax.div(ids, 4 * ny)
    off = lax.rem(home_y - my + ny, ny)
    last = (off == 0) | (off == half)
    pair = jnp.where(last, half - 1, jnp.where(off < half, off - 1, ny - 1 - off))
    side = jnp.where(off < half, 0, 1)
    at = (lax.div(pair, nb) * nq + home_x * 2 + core) * span
    at = at + (lax.rem(pair, nb) * 2 + side) * 2 * CAP + second * CAP
    slot = at.astype(F32) + rank
    total = BATCHES * nq * span
    place[...] = (lax.broadcasted_iota(jnp.int32, (total, rows), 0).astype(F32) == slot).astype(F32).astype(BF16)

    pl.semaphore_wait(barrier, nq + nz)

    below = [(d, j) for d in range(1, half) for j in (0, 1)] + [(half, 0)]
    above = [(d, 1 - j) for d, j in below]

    def y_copy(n, way):
        d, j = (below if way > 0 else above)[n]
        src, dst = (-(d - 1) * way) % ny, (-d * way) % ny
        return remote(panels.at[src, j], panels.at[dst, j], y_ss.at[n, (1 - way) // 2], y_rs.at[n, (1 - way) // 2],
                      along_y(way))

    loads[0].wait()
    loads[1].wait()
    order = [(d, j) for d, j in below]

    def y_start(n):
        y_copy(n, 1).start()
        y_copy(n, -1).start()

    def y_step(n):
        y_copy(n, 1).wait_recv()
        y_copy(n, -1).wait_recv()
        if n + 2 < len(order):
            y_start(n + 2)
        elif n + 2 == len(order):
            pass

    y_start(0)
    y_start(1)

    loads[2].wait()
    cols = min(256, width)
    for c in range(width // cols):
        g = jnp.dot(place[...], tok[:, c * cols:(c + 1) * cols], preferred_element_type=F32)
        send[:, :, :, c * cols:(c + 1) * cols] = g.reshape(BATCHES, nq, span, cols).astype(BF16)

    def x_copy(n, at_q, q):
        b = lax.div(n, nq - 1)
        return remote(send.at[b, q], recv.at[b, at_q], x_ss.at[n], x_rs.at[n], along_x(q))

    @pl.loop(0, BATCHES * (nq - 1))
    def _(n):
        x_copy(n, mq, lax.rem(mq + lax.rem(n, nq - 1) + 1, nq)).start()

    for b in range(BATCHES):
        recv[b, mq] = send[b, mq]

    loads[3].wait()
    for c in range(nz // 2):
        g = jnp.dot(tok[...], w[:, c * 2 * feat:(c + 1) * 2 * feat], preferred_element_type=F32)
        part[2 * c] = g[:, :feat]
        part[2 * c + 1] = g[:, feat:]

    def z_copy(s, way):
        k = (1 - way) // 2
        return remote(zs.at[k, s], zr.at[k, s], z_ss.at[k, s], z_rs.at[k, s], along_z(lax.rem(t + way + nz, nz)))

    def z_step(s):
        for way, hops in ((1, hz), (-1, hz - 1)):
            if s >= hops:
                continue
            k = (1 - way) // 2
            v = part[lax.rem(t + way * (hops - s) + nz, nz)]
            if s > 0:
                z_copy(s - 1, way).wait_recv()
                v = v + zr[k, s - 1].astype(F32)
            zs[k, s] = v.astype(BF16)
            z_copy(s, way).start()

    top = lax.broadcasted_iota(jnp.int32, (nx, 2 * CAP, 2 * rk), 1) < CAP
    first = lax.broadcasted_iota(jnp.int32, (nx, 2 * CAP, 2 * rk), 2) < rk

    def swap(v):
        return jnp.concatenate([v[:, CAP:], v[:, :CAP]], axis=1)

    def offsets(m):
        return (0, half) if m == half - 1 else (m + 1, ny - 1 - m)

    def x_wait(b):
        @pl.loop(0, nq - 1)
        def _(n):
            x_copy(b * (nq - 1) + n, mq, mq).wait_recv()

    def rank_part(b, mm):
        e0, e1 = offsets(b * nb + mm)
        down = jnp.concatenate([panels[e, j, :, :width] for e in (e0, e1) for j in (0, 1)], axis=0)
        x = recv[b, :, mm * 4 * CAP:(mm + 1) * 4 * CAP, :].reshape(nq * 4 * CAP, width)
        r = lax.dot_general(x, down, (((1,), (1,)), ((), ())), preferred_element_type=F32)
        r = r.reshape(nq, 4 * CAP, 4 * rk)
        for e in (0, 1):
            v = r[:, e * 2 * CAP:(e + 1) * 2 * CAP, e * 2 * rk:(e + 1) * 2 * rk].reshape(nx, 2, 2 * CAP, 2 * rk)
            even, odd = v[:, 0], v[:, 1]
            packed = jnp.where(top, jnp.where(first, even, swap(even)), jnp.where(first, swap(odd), odd))
            for i in range(nx):
                rsend[b, 2 * i + e, mm] = packed[i]

    def sum_copy(b, p, at_p):
        return remote(rsend.at[b, p], rrecv.at[b, at_p], r_ss.at[b, p], r_rs.at[b, at_p], along_z(p))

    def sum_start(b):
        @pl.loop(1, nz)
        def _(j):
            sum_copy(b, lax.rem(t + j, nz), t).start()

        rrecv[b, t] = rsend[b, t]

    def full_copy(b, p, at_p):
        return remote(full.at[b, at_p], full.at[b, at_p], a_ss.at[b, p], a_rs.at[b, at_p], along_z(p))

    def full_start(b):
        @pl.loop(1, nz)
        def _(j):
            p = lax.rem(t + j, nz)
            sum_copy(b, p, p).wait_recv()

        v = rrecv[b, 0]
        for p in range(1, nz):
            v = v + rrecv[b, p]
        full[b, t] = v

        @pl.loop(1, nz)
        def _(j):
            full_copy(b, lax.rem(t + j, nz), t).start()

    def lora_copy(b, q, at_q):
        return remote(lsend.at[b, q], lrecv.at[b, at_q], l_ss.at[b, q], l_rs.at[b, at_q], along_x(q))

    def lora_start(b):
        @pl.loop(1, nz)
        def _(j):
            p = lax.rem(t + j, nz)
            full_copy(b, p, p).wait_recv()

        tiles = full[b].reshape(nx, 2, nb, 2 * CAP, 2 * rk)
        zero = jnp.zeros((nx, 2 * CAP, 2 * rk), F32)
        for mm in range(nb):
            for side_at, e in enumerate(offsets(b * nb + mm)):
                v = tiles[:, side_at, mm]
                other = swap(v)
                even = jnp.where(top, jnp.where(first, v, zero), jnp.where(first, zero, other))
                odd = jnp.where(top, jnp.where(first, other, zero), jnp.where(first, zero, v))
                lhs = jnp.concatenate([even[:, None], odd[:, None]], axis=1).reshape(nq * 2 * CAP, 2 * rk)
                high = lhs.astype(BF16)
                low = (lhs - high.astype(F32)).astype(BF16)
                ups = jnp.concatenate([panels[e, j, :, width:] for j in (0, 1)] * 2, axis=0)
                g = jnp.dot(jnp.concatenate([high, low], axis=1), ups, preferred_element_type=F32)
                g = g.reshape(nq, 2 * CAP, feat)
                if side_at == 0:
                    kept = g
                else:
                    lsend[b, :, mm * 4 * CAP:(mm + 1) * 4 * CAP, :] = jnp.concatenate([kept, g], axis=1).astype(BF16)

        @pl.loop(1, nq)
        def _(j):
            lora_copy(b, lax.rem(mq + j, nq), mq).start()

        lrecv[b, mq] = lsend[b, mq]

    def lora_add(b):
        @pl.loop(1, nq)
        def _(j):
            q = lax.rem(mq + j, nq)
            lora_copy(b, q, q).wait_recv()

        back = lrecv[b].reshape(nq * span, feat)
        return lax.dot_general(back, place[b * nq * span:(b + 1) * nq * span, :], (((0,), (0,)), ((), ())),
                               preferred_element_type=F32)

    ready = [2 * nb * (b + 1) - 1 for b in range(BATCHES - 1)] + [len(order) - 1]
    for n in range(ready[0] + 1):
        if n < hz:
            z_step(n)
        y_step(n)
    x_wait(0)
    for mm in range(nb):
        rank_part(0, mm)
    sum_start(0)
    x_wait(1)
    for n in range(ready[0] + 1, len(order) - 1):
        y_step(n)
    for s in range(ready[0] + 1, hz):
        z_step(s)
    full_start(0)
    for mm in range(nb - 1):
        rank_part(1, mm)
    acc = part[t]
    for way, hops in ((1, hz), (-1, hz - 1)):
        z_copy(hops - 1, way).wait_recv()
        acc = acc + zr[(1 - way) // 2, hops - 1].astype(F32)
    acc = acc.T
    lora_start(0)
    y_step(len(order) - 1)
    rank_part(1, nb - 1)
    sum_start(1)
    acc = acc + lora_add(0)
    full_start(1)
    lora_start(1)
    out_ref[...] = (acc + lora_add(1)).astype(BF16)

    for n in range(len(order)):
        y_copy(n, 1).wait_send()
        y_copy(n, -1).wait_send()

    @pl.loop(0, BATCHES * (nq - 1))
    def _(n):
        x_copy(n, mq, mq).wait_send()

    for way, hops in ((1, hz), (-1, hz - 1)):
        for s in range(hops):
            z_copy(s, way).wait_send()
    for b in range(BATCHES):
        @pl.loop(1, nz)
        def _(j):
            p = lax.rem(t + j, nz)
            sum_copy(b, p, t).wait_send()
            full_copy(b, p, t).wait_send()

        @pl.loop(1, nq)
        def _(j):
            lora_copy(b, lax.rem(mq + j, nq), mq).wait_send()


def local(dims, tokens, w_key, row_adapter, panel_a, up_panels):
    nx, ny, nz = dims
    rows, width = tokens.shape
    feat = w_key.shape[1] // nz
    rk = panel_a.shape[2]
    nq, half, hz = 2 * nx, ny // 2, nz // 2
    nb = half // BATCHES
    span = nb * 4 * CAP
    vmem = pl.BlockSpec(memory_space=pltpu.VMEM)
    hbm = pl.BlockSpec(memory_space=pl.ANY)
    dma = pltpu.SemaphoreType.DMA
    tiles = (BATCHES, nz, nb, 2 * CAP, 2 * rk)
    return pl.pallas_call(
        functools.partial(kernel, dims),
        out_shape=jax.ShapeDtypeStruct((feat, rows), BF16),
        in_specs=[vmem, hbm, hbm, hbm, hbm],
        out_specs=vmem,
        scratch_shapes=[
            pltpu.VMEM((rows, width), BF16),
            pltpu.VMEM(w_key.shape, BF16),
            pltpu.VMEM((ny, 2, rk, width + feat), BF16),
            pltpu.VMEM((BATCHES * nq * span, rows), BF16),
            pltpu.VMEM((BATCHES, nq, span, width), BF16),
            pltpu.VMEM((BATCHES, nq, span, width), BF16),
            pltpu.VMEM((nz, rows, feat), F32),
            pltpu.VMEM((2, hz, rows, feat), BF16),
            pltpu.VMEM((2, hz, rows, feat), BF16),
            pltpu.VMEM(tiles, F32),
            pltpu.VMEM(tiles, F32),
            pltpu.VMEM(tiles, F32),
            pltpu.VMEM((BATCHES, nq, span, feat), BF16),
            pltpu.VMEM((BATCHES, nq, span, feat), BF16),
            dma((4,)),
            dma((ny - 1, 2)),
            dma((ny - 1, 2)),
            dma((BATCHES * (nq - 1),)),
            dma((BATCHES * (nq - 1),)),
            dma((2, hz)),
            dma((2, hz)),
            dma((BATCHES, nz)),
            dma((BATCHES, nz)),
            dma((BATCHES, nz)),
            dma((BATCHES, nz)),
            dma((BATCHES, nq)),
            dma((BATCHES, nq)),
        ],
        compiler_params=pltpu.CompilerParams(
            collective_id=0, has_side_effects=True, vmem_limit_bytes=62 * 1024 * 1024),
    )(row_adapter.reshape(1, rows), tokens, w_key, jnp.swapaxes(panel_a, 1, 2), up_panels)


def solution(mesh):
    return jax.shard_map(
        functools.partial(local, (X, Y, mesh.shape["tensor"])),
        mesh=mesh,
        in_specs=(
            P("group", "tensor"),
            P("tensor", None),
            P("group", None),
            P("group", "tensor", None),
            P("group", None, None),
        ),
        out_specs=P("tensor", "group"),
        check_vma=False,
    )
```

time: 165 us -> 61.1 us (0.37)
  the two profiles are of different devices: /device:TPU:6 before, /device:TPU:1 now
where the time goes in v2:
time: 61.1 us; the launch traced here: 60.9 us
  Pallas kernels  59.4 us (97%)
  local copies, waits for them, and re-layouts  1.54 us (3%)
    pallas_call x1, Pallas kernels, local(): pl.pallas_call(functools.partial(kernel, dims), out_shape=jax.ShapeDtypeS...  59.4 us
    unnamed x1, local copies, waits for them, and re-layouts  1.54 us

profile of v2, /device:TPU:1, one launch (start us, length us, event | category | flops | bytes accessed | tf_op | source)
XLA Modules:
  0.0 60.9 jit_solution(15020300611021177478)
XLA Ops:
  0.0 59.4 %shard_map.55 = bf16[128,384]{1,0:T(8,128)(2,1)} custom-call(s32[1,384]{1,0:T(1,128)} %bitcast.3, bf16[384,1024]{1,0:T(8,128)(2,1)} %tok_hbm.1, bf16[1024,1024]{1,0:T(8,128)(2,1)} %w_hbm.1, bf16[2,64,1024]{2,1,0:T(8,128)(2,1)} %bitcast.2, bf16[2,64,1024]{2,1,0:T(8,128)(2,1)} %up_hbm.1), custom_call_target="tpu_custom_call" | custom-call | tf_op jit(solution)/shard_map/pallas_call | solution.py:319
  59.4 1.5 %copy.7 = bf16[128,384]{1,0:T(8,128)(2,1)} copy(bf16[128,384]{1,0:T(8,128)(2,1)} %shard_map.55) | data formatting | bytes 196608

commit v3 on v0

v3 whole, which is shorter than its diff:
```python
import functools

import jax
import jax.numpy as jnp
from jax import lax
from jax.experimental import pallas as pl
from jax.experimental.pallas import tpu as pltpu
from jax.sharding import PartitionSpec as P

MESH = pl.DeviceIdType.MESH
F32, BF16 = jnp.float32, jnp.bfloat16
X, Y = 4, 8
CAP = 4

def batches(ny):
    half = ny // 2
    over_z = [[0, 1, ny - 1]] + [[d, ny - d] for d in range(2, half)] + [[half]]
    early = [e for d in range(1, half - 1) for e in (d, ny - d)]
    back = ([early] if early else []) + [[half - 1, half + 1], [0, half]]
    return over_z, back


def kernel(dims, ids_ref, tok_hbm, w_hbm, pa_hbm, up_hbm, out_ref,
           tok, w, panels, place, send, recv, part, zs, zr, rsend, rrecv, rown, widened, lsend, lrecv,
           in_sem, y_ss, y_rs, x_ss, x_rs, z_ss, z_rs, r_ss, r_rs, l_ss, l_rs):
    nx, ny, nz = dims
    nq = 2 * nx
    half, hz = ny // 2, nz // 2
    rows, width = tok.shape
    feat = out_ref.shape[0]
    rk = panels.shape[2]
    slots = 2 * CAP
    over_z, back = batches(ny)
    order = [e for b in over_z for e in b]
    begin, where_back = [], {}
    for b, offs in enumerate(back):
        begin.append(sum(len(o) for o in back[:b]) * nq * slots)
        for i, e in enumerate(offs):
            where_back[e] = (b, i)

    me, t = lax.axis_index("group"), lax.axis_index("tensor")
    mc, my, mx = lax.rem(me, 2), lax.rem(lax.div(me, 2), ny), lax.div(me, 2 * ny)
    mq = mx * 2 + mc

    def along_x(q):
        return {"group": (lax.div(q, 2) * ny + my) * 2 + lax.rem(q, 2)}

    def along_y(step):
        return {"group": (mx * ny + lax.rem(my + step + ny, ny)) * 2 + mc}

    def along_z(p):
        return {"tensor": p}

    def remote(src, dst, ss, rs, where):
        return pltpu.make_async_remote_copy(src, dst, ss, rs, device_id=where, device_id_type=MESH)

    barrier = pltpu.get_barrier_semaphore()
    for step in (-1, 1):
        pl.semaphore_signal(barrier, inc=1, device_id=along_y(step), device_id_type=MESH)

    mine = pl.ds(pl.multiple_of(t * feat, feat), feat)
    loads = [
        pltpu.make_async_copy(pa_hbm, panels.at[0, :, :, pl.ds(0, width)], in_sem.at[0]),
        pltpu.make_async_copy(up_hbm.at[:, :, mine], panels.at[0, :, :, pl.ds(width, feat)], in_sem.at[1]),
        pltpu.make_async_copy(tok_hbm, tok, in_sem.at[2]),
        pltpu.make_async_copy(w_hbm, w, in_sem.at[3]),
    ]
    for c in loads:
        c.start()

    @pl.loop(1, nq)
    def _(j):
        pl.semaphore_signal(barrier, inc=1, device_id=along_x(lax.rem(mq + j, nq)), device_id_type=MESH)

    @pl.loop(1, nz)
    def _(j):
        pl.semaphore_signal(barrier, inc=1, device_id=along_z(lax.rem(t + j, nz)), device_id_type=MESH)

    pl.semaphore_wait(barrier, nq + nz)

    below = [(d, j) for d in range(1, half) for j in (0, 1)] + [(half, 0)]
    above = [(d, 1 - j) for d, j in below]
    steps = len(below)

    def y_copy(n, way):
        d, j = (below if way > 0 else above)[n]
        src, dst = (-(d - 1) * way) % ny, (-d * way) % ny
        return remote(panels.at[src, j], panels.at[dst, j], y_ss.at[n, (1 - way) // 2], y_rs.at[n, (1 - way) // 2],
                      along_y(way))

    def y_step(n):
        for way in (1, -1):
            y_copy(n, way).wait_recv()
            if n + 2 < steps:
                y_copy(n + 2, way).start()

    loads[0].wait()
    loads[1].wait()
    for n in (0, 1):
        y_copy(n, 1).start()
        y_copy(n, -1).start()

    ids = ids_ref[...]
    one_hot = (lax.broadcasted_iota(jnp.int32, (2 * nq * ny, rows), 0) == ids).astype(F32)
    earlier = (lax.broadcasted_iota(jnp.int32, (rows, rows), 0)
               < lax.broadcasted_iota(jnp.int32, (rows, rows), 1)).astype(F32).astype(BF16)
    before = jnp.dot(one_hot.astype(BF16), earlier, preferred_element_type=F32)
    rank = jnp.sum(before * one_hot, axis=0, keepdims=True)
    second, core = lax.rem(ids, 2), lax.rem(lax.div(ids, 2), 2)
    home_y, home_x = lax.rem(lax.div(ids, 4), ny), lax.div(ids, 4 * ny)
    off = lax.rem(home_y - my + ny, ny)
    at = second * CAP
    for e, (b, i) in where_back.items():
        at = at + jnp.where(off == e, begin[b] + i * slots + (home_x * 2 + core) * (len(back[b]) * slots), 0)
    slot = at.astype(F32) + rank
    total = place.shape[0]
    place[...] = (lax.broadcasted_iota(jnp.int32, (total, rows), 0).astype(F32) == slot).astype(F32).astype(BF16)

    loads[2].wait()
    cols = min(256, width)
    for c in range(width // cols):
        send[:, c * cols:(c + 1) * cols] = jnp.dot(
            place[...], tok[:, c * cols:(c + 1) * cols], preferred_element_type=F32).astype(BF16)

    def block(b, q):
        span = len(back[b]) * slots
        return pl.ds(pl.multiple_of(begin[b] + q * span, span), span)

    def x_copy(b, q, at_q):
        return remote(send.at[block(b, q)], recv.at[block(b, at_q)], x_ss.at[b, q], x_rs.at[b, at_q], along_x(q))

    for b in range(len(back)):
        @pl.loop(1, nq)
        def _(j):
            x_copy(b, lax.rem(mq + j, nq), mq).start()

        recv[block(b, mq)] = send[block(b, mq)]

    def base_parts():
        loads[3].wait()
        for c in range(nz // 2):
            g = jnp.dot(tok[...], w[:, c * 2 * feat:(c + 1) * 2 * feat], preferred_element_type=F32)
            part[2 * c] = g[:, :feat]
            part[2 * c + 1] = g[:, feat:]

    def z_copy(s, way):
        k = (1 - way) // 2
        return remote(zs.at[k, s], zr.at[k, s], z_ss.at[k, s], z_rs.at[k, s], along_z(lax.rem(t + way + nz, nz)))

    def z_step(s):
        for way, hops in ((1, hz), (-1, hz - 1)):
            if s >= hops:
                continue
            k = (1 - way) // 2
            v = part[lax.rem(t + way * (hops - s) + nz, nz)]
            if s > 0:
                z_copy(s - 1, way).wait_recv()
                v = v + zr[k, s - 1].astype(F32)
            zs[k, s] = v.astype(BF16)
            z_copy(s, way).start()

    top = lax.broadcasted_iota(jnp.int32, (nx, slots, 2 * rk), 1) < CAP
    first = lax.broadcasted_iota(jnp.int32, (nx, slots, 2 * rk), 2) < rk

    def swap(v):
        return jnp.concatenate([v[:, CAP:], v[:, :CAP]], axis=1)

    def x_wait(b):
        @pl.loop(1, nq)
        def _(j):
            q = lax.rem(mq + j, nq)
            x_copy(b, q, q).wait_recv()

    def rank_part(offs):
        b, i = where_back[offs[0]]
        lo = i // 2 * 2 * slots
        span = len(back[b]) * slots
        x = recv[begin[b]:begin[b] + nq * span, :].reshape(nq, span, width)[:, lo:lo + 2 * slots]
        x = x.reshape(nq * 2 * slots, width)
        down = jnp.concatenate([panels[e, j, :, :width] for e in offs for j in (0, 1)], axis=0)
        r = lax.dot_general(x, down, (((1,), (1,)), ((), ())), preferred_element_type=F32)
        r = r.reshape(nq, 2 * slots, len(offs) * 2 * rk)
        for n, e in enumerate(offs):
            s = where_back[e][1] % 2
            v = r[:, s * slots:(s + 1) * slots, n * 2 * rk:(n + 1) * 2 * rk].reshape(nx, 2, slots, 2 * rk)
            even, odd = v[:, 0], v[:, 1]
            packed = jnp.where(top, jnp.where(first, even, swap(even)), jnp.where(first, swap(odd), odd))
            packed = packed.reshape(nx * slots, 2 * rk)
            rown[order.index(e)] = packed
            rsend[order.index(e)] = packed.astype(BF16)

    def these(b):
        return pl.ds(order.index(over_z[b][0]), len(over_z[b]))

    def rank_copy(b, p, at_p):
        return remote(rsend.at[these(b)], rrecv.at[at_p, these(b)], r_ss.at[b, p], r_rs.at[b, at_p], along_z(p))

    def rank_send(b):
        pairs = [over_z[b][:1], over_z[b][1:]] if len(over_z[b]) % 2 else [over_z[b]]
        for offs in pairs:
            if offs:
                rank_part(offs)

        @pl.loop(1, nz)
        def _(j):
            rank_copy(b, lax.rem(t + j, nz), t).start()

        rrecv[t, these(b)] = jnp.zeros((len(over_z[b]), nx * slots, 2 * rk), BF16)

    def lora_copy(b, q, at_q):
        return remote(lsend.at[block(b, q)], lrecv.at[block(b, at_q)], l_ss.at[b, q], l_rs.at[b, at_q], along_x(q))

    def widen(b):
        @pl.loop(1, nz)
        def _(j):
            p = lax.rem(t + j, nz)
            rank_copy(b, p, p).wait_recv()

        for e in over_z[b]:
            n = order.index(e)
            v = rown[n]
            for p in range(nz):
                v = v + rrecv[p, n].astype(F32)
            v = v.reshape(nx, slots, 2 * rk)
            zero = jnp.zeros_like(v)
            other = swap(v)
            even = jnp.where(top, jnp.where(first, v, zero), jnp.where(first, zero, other))
            odd = jnp.where(top, jnp.where(first, other, zero), jnp.where(first, zero, v))
            lhs = jnp.concatenate([even[:, None], odd[:, None]], axis=1).reshape(nq * slots, 2 * rk)
            high = lhs.astype(BF16)
            low = (lhs - high.astype(F32)).astype(BF16)
            ups = jnp.concatenate([panels[e, j, :, width:] for j in (0, 1)] * 2, axis=0)
            g = jnp.dot(jnp.concatenate([high, low], axis=1), ups, preferred_element_type=F32)
            widened[e] = g.reshape(nq, slots, feat)
        done = [e for o in over_z[:b + 1] for e in o]
        for k, offs in enumerate(back):
            if set(offs) <= set(done) and not set(offs) <= set(done) - set(over_z[b]):
                g = jnp.concatenate([widened[e] for e in offs], axis=1).astype(BF16)
                lsend[begin[k]:begin[k] + nq * len(offs) * slots, :] = g.reshape(nq * len(offs) * slots, feat)

                @pl.loop(1, nq)
                def _(j):
                    lora_copy(k, lax.rem(mq + j, nq), mq).start()

                lrecv[block(k, mq)] = lsend[block(k, mq)]

    def lora_add(b):
        @pl.loop(1, nq)
        def _(j):
            q = lax.rem(mq + j, nq)
            lora_copy(b, q, q).wait_recv()

        lo, n = begin[b], nq * len(back[b]) * slots
        return lax.dot_general(lrecv[lo:lo + n, :], place[lo:lo + n, :], (((0,), (0,)), ((), ())),
                               preferred_element_type=F32)

    last = len(over_z) - 1
    z_at = {0: 0, 2: 1, 4: 2, 5: 3}
    z_done = w_done = 0
    for n in range(steps):
        y_step(n)
        if n == 0:
            base_parts()
        if n in z_at and z_at[n] < hz:
            z_step(z_at[n])
            z_done = z_at[n] + 1
        if n == 1:
            for b in range(len(back)):
                x_wait(b)
        if n % 2 == 1:
            rank_send(n // 2)
        if n >= 4 and n < steps - 1:
            widen(w_done)
            w_done += 1
    rank_send(last)
    for s in range(z_done, hz):
        z_step(s)
    acc = part[t]
    for way, hops in ((1, hz), (-1, hz - 1)):
        z_copy(hops - 1, way).wait_recv()
        acc = acc + zr[(1 - way) // 2, hops - 1].astype(F32)
    acc = acc.T
    for b in range(w_done, last):
        widen(b)
    if len(back) > 2:
        acc = acc + lora_add(0)
    widen(last)
    acc = acc + lora_add(len(back) - 2)
    out_ref[...] = (acc + lora_add(len(back) - 1)).astype(BF16)

    for n in range(steps):
        y_copy(n, 1).wait_send()
        y_copy(n, -1).wait_send()
    for way, hops in ((1, hz), (-1, hz - 1)):
        for s in range(hops):
            z_copy(s, way).wait_send()
    for b in range(len(back)):
        @pl.loop(1, nq)
        def _(j):
            q = lax.rem(mq + j, nq)
            x_copy(b, q, mq).wait_send()
            lora_copy(b, q, mq).wait_send()
    for b in range(len(over_z)):
        @pl.loop(1, nz)
        def _(j):
            rank_copy(b, lax.rem(t + j, nz), t).wait_send()


def local(dims, tokens, w_key, row_adapter, panel_a, up_panels):
    nx, ny, nz = dims
    rows, width = tokens.shape
    feat = w_key.shape[1] // nz
    rk = panel_a.shape[2]
    nq, hz = 2 * nx, nz // 2
    over_z, back = batches(ny)
    total = ny * nq * 2 * CAP
    vmem = pl.BlockSpec(memory_space=pltpu.VMEM)
    hbm = pl.BlockSpec(memory_space=pl.ANY)
    dma = pltpu.SemaphoreType.DMA
    tiles = (ny, nx * 2 * CAP, 2 * rk)
    return pl.pallas_call(
        functools.partial(kernel, dims),
        out_shape=jax.ShapeDtypeStruct((feat, rows), BF16),
        in_specs=[vmem, hbm, hbm, hbm, hbm],
        out_specs=vmem,
        scratch_shapes=[
            pltpu.VMEM((rows, width), BF16),
            pltpu.VMEM(w_key.shape, BF16),
            pltpu.VMEM((ny, 2, rk, width + feat), BF16),
            pltpu.VMEM((total, rows), BF16),
            pltpu.VMEM((total, width), BF16),
            pltpu.VMEM((total, width), BF16),
            pltpu.VMEM((nz, rows, feat), F32),
            pltpu.VMEM((2, hz, rows, feat), BF16),
            pltpu.VMEM((2, hz, rows, feat), BF16),
            pltpu.VMEM(tiles, BF16),
            pltpu.VMEM((nz, *tiles), BF16),
            pltpu.VMEM(tiles, F32),
            pltpu.VMEM((ny, nq, 2 * CAP, feat), F32),
            pltpu.VMEM((total, feat), BF16),
            pltpu.VMEM((total, feat), BF16),
            dma((4,)),
            dma((ny - 1, 2)),
            dma((ny - 1, 2)),
            dma((len(back), nq)),
            dma((len(back), nq)),
            dma((2, hz)),
            dma((2, hz)),
            dma((len(over_z), nz)),
            dma((len(over_z), nz)),
            dma((len(back), nq)),
            dma((len(back), nq)),
        ],
        compiler_params=pltpu.CompilerParams(
            collective_id=0, has_side_effects=True, vmem_limit_bytes=62 * 1024 * 1024),
    )(row_adapter.reshape(1, rows), tokens, w_key, jnp.swapaxes(panel_a, 1, 2), up_panels)


def solution(mesh):
    return jax.shard_map(
        functools.partial(local, (X, Y, mesh.shape["tensor"])),
        mesh=mesh,
        in_specs=(
            P("group", "tensor"),
            P("tensor", None),
            P("group", None),
            P("group", "tensor", None),
            P("group", None, None),
        ),
        out_specs=P("tensor", "group"),
        check_vma=False,
    )
```

time: 165 us -> 61.4 us (0.37)
  the two profiles are of different devices: /device:TPU:6 before, /device:TPU:1 now
where the time goes in v3:
time: 61.4 us; the launch traced here: 61.3 us
  Pallas kernels  59.7 us (97%)
  local copies, waits for them, and re-layouts  1.54 us (3%)
    pallas_call x1, Pallas kernels, local(): pl.pallas_call(functools.partial(kernel, dims), out_shape=jax.ShapeDtypeS...  59.7 us
    unnamed x1, local copies, waits for them, and re-layouts  1.54 us

profile of v3, /device:TPU:1, one launch (start us, length us, event | category | flops | bytes accessed | tf_op | source)
XLA Modules:
  0.0 61.3 jit_solution(16784305038145141195)
XLA Ops:
  0.0 59.7 %shard_map.55 = bf16[128,384]{1,0:T(8,128)(2,1)} custom-call(s32[1,384]{1,0:T(1,128)} %bitcast.3, bf16[384,1024]{1,0:T(8,128)(2,1)} %tok_hbm.1, bf16[1024,1024]{1,0:T(8,128)(2,1)} %w_hbm.1, bf16[2,64,1024]{2,1,0:T(8,128)(2,1)} %bitcast.2, bf16[2,64,1024]{2,1,0:T(8,128)(2,1)} %up_hbm.1), custom_call_target="tpu_custom_call" | custom-call | tf_op jit(solution)/shard_map/pallas_call | solution.py:321
  59.7 1.5 %copy.7 = bf16[128,384]{1,0:T(8,128)(2,1)} copy(bf16[128,384]{1,0:T(8,128)(2,1)} %shard_map.55) | data formatting | bytes 196608

commit v4 on v3

--- a/solution.py
+++ b/solution.py
@@ -14,18 +14,18 @@
 
 def batches(ny):
     half = ny // 2
-    over_z = [[0, 1, ny - 1]] + [[d, ny - d] for d in range(2, half)] + [[half]]
+    over_z = [[d, ny - d] for d in range(1, half - 1)] + [[0, half - 1, half + 1], [half]]
     early = [e for d in range(1, half - 1) for e in (d, ny - d)]
     back = ([early] if early else []) + [[half - 1, half + 1], [0, half]]
     return over_z, back
 
 
-def kernel(dims, ids_ref, tok_hbm, w_hbm, pa_hbm, up_hbm, out_ref,
-           tok, w, panels, place, send, recv, part, zs, zr, rsend, rrecv, rown, widened, lsend, lrecv,
+def kernel(dims, ids_hbm, tok_hbm, w_hbm, pa_hbm, up_hbm, out_ref,
+           ids_ref, tok, w, panels, place, send, recv, part, zs, zr, rsend, rrecv, rown, widened, lsend, lrecv,
            in_sem, y_ss, y_rs, x_ss, x_rs, z_ss, z_rs, r_ss, r_rs, l_ss, l_rs):
     nx, ny, nz = dims
     nq = 2 * nx
-    half, hz = ny // 2, nz // 2
+    half = ny // 2
     rows, width = tok.shape
     feat = out_ref.shape[0]
     rk = panels.shape[2]
@@ -63,6 +63,7 @@
         pltpu.make_async_copy(pa_hbm, panels.at[0, :, :, pl.ds(0, width)], in_sem.at[0]),
         pltpu.make_async_copy(up_hbm.at[:, :, mine], panels.at[0, :, :, pl.ds(width, feat)], in_sem.at[1]),
         pltpu.make_async_copy(tok_hbm, tok, in_sem.at[2]),
+        pltpu.make_async_copy(ids_hbm, ids_ref, in_sem.at[4]),
         pltpu.make_async_copy(w_hbm, w, in_sem.at[3]),
     ]
     for c in loads:
@@ -100,6 +101,7 @@
         y_copy(n, 1).start()
         y_copy(n, -1).start()
 
+    loads[3].wait()
     ids = ids_ref[...]
     one_hot = (lax.broadcasted_iota(jnp.int32, (2 * nq * ny, rows), 0) == ids).astype(F32)
     earlier = (lax.broadcasted_iota(jnp.int32, (rows, rows), 0)
@@ -137,27 +139,35 @@
         recv[block(b, mq)] = send[block(b, mq)]
 
     def base_parts():
-        loads[3].wait()
+        loads[4].wait()
         for c in range(nz // 2):
             g = jnp.dot(tok[...], w[:, c * 2 * feat:(c + 1) * 2 * feat], preferred_element_type=F32)
             part[2 * c] = g[:, :feat]
             part[2 * c + 1] = g[:, feat:]
 
-    def z_copy(s, way):
-        k = (1 - way) // 2
-        return remote(zs.at[k, s], zr.at[k, s], z_ss.at[k, s], z_rs.at[k, s], along_z(lax.rem(t + way + nz, nz)))
-
-    def z_step(s):
-        for way, hops in ((1, hz), (-1, hz - 1)):
-            if s >= hops:
-                continue
-            k = (1 - way) // 2
-            v = part[lax.rem(t + way * (hops - s) + nz, nz)]
-            if s > 0:
-                z_copy(s - 1, way).wait_recv()
-                v = v + zr[k, s - 1].astype(F32)
-            zs[k, s] = v.astype(BF16)
-            z_copy(s, way).start()
+    turn = 1 - 2 * lax.rem(t, 2)
+
+    def at_z(step):
+        return lax.rem(t + step * turn + nz, nz)
+
+    def z_copy(n):
+        to = (2, -1, 1, -1, 1, 2, -2)[n]
+        return remote(zs.at[n], zr.at[n], z_ss.at[n], z_rs.at[n], along_z(at_z(to)))
+
+    def z_send(n, v):
+        zs[n] = v.astype(BF16)
+        z_copy(n).start()
+
+    def z_first():
+        for n, target in enumerate((4, -3, 3, -1, 1)):
+            z_send(n, part[at_z(target)])
+
+    def z_second():
+        z_copy(0).wait_recv()
+        z_copy(1).wait_recv()
+        z_send(5, part[at_z(2)] + zr[0].astype(F32) + zr[1].astype(F32))
+        z_copy(2).wait_recv()
+        z_send(6, part[at_z(-2)] + zr[2].astype(F32))
 
     top = lax.broadcasted_iota(jnp.int32, (nx, slots, 2 * rk), 1) < CAP
     first = lax.broadcasted_iota(jnp.int32, (nx, slots, 2 * rk), 2) < rk
@@ -255,45 +265,37 @@
                                preferred_element_type=F32)
 
     last = len(over_z) - 1
-    z_at = {0: 0, 2: 1, 4: 2, 5: 3}
-    z_done = w_done = 0
+    waited = -1
     for n in range(steps):
         y_step(n)
         if n == 0:
             base_parts()
-        if n in z_at and z_at[n] < hz:
-            z_step(z_at[n])
-            z_done = z_at[n] + 1
-        if n == 1:
-            for b in range(len(back)):
-                x_wait(b)
-        if n % 2 == 1:
-            rank_send(n // 2)
-        if n >= 4 and n < steps - 1:
-            widen(w_done)
-            w_done += 1
-    rank_send(last)
-    for s in range(z_done, hz):
-        z_step(s)
+            z_first()
+        if n == steps // 2:
+            z_second()
+        b = {2: 0, 3: 1, 5: 2, 6: 3}.get(n) if steps == 7 else {1: 0, 2: 1}.get(n)
+        if b is not None:
+            need = max(where_back[e][0] for e in over_z[b])
+            while waited < need:
+                waited += 1
+                x_wait(waited)
+            rank_send(b)
     acc = part[t]
-    for way, hops in ((1, hz), (-1, hz - 1)):
-        z_copy(hops - 1, way).wait_recv()
-        acc = acc + zr[(1 - way) // 2, hops - 1].astype(F32)
+    for n in (3, 4, 5, 6):
+        z_copy(n).wait_recv()
+        acc = acc + zr[n].astype(F32)
     acc = acc.T
-    for b in range(w_done, last):
+    for b in range(last + 1):
         widen(b)
-    if len(back) > 2:
-        acc = acc + lora_add(0)
-    widen(last)
-    acc = acc + lora_add(len(back) - 2)
-    out_ref[...] = (acc + lora_add(len(back) - 1)).astype(BF16)
+    for b in range(len(back)):
+        acc = acc + lora_add(b)
+    out_ref[...] = acc.astype(BF16)
 
     for n in range(steps):
         y_copy(n, 1).wait_send()
         y_copy(n, -1).wait_send()
-    for way, hops in ((1, hz), (-1, hz - 1)):
-        for s in range(hops):
-            z_copy(s, way).wait_send()
+    for n in range(7):
+        z_copy(n).wait_send()
     for b in range(len(back)):
         @pl.loop(1, nq)
         def _(j):
@@ -311,7 +313,7 @@
     rows, width = tokens.shape
     feat = w_key.shape[1] // nz
     rk = panel_a.shape[2]
-    nq, hz = 2 * nx, nz // 2
+    nq = 2 * nx
     over_z, back = batches(ny)
     total = ny * nq * 2 * CAP
     vmem = pl.BlockSpec(memory_space=pltpu.VMEM)
@@ -321,9 +323,10 @@
     return pl.pallas_call(
         functools.partial(kernel, dims),
         out_shape=jax.ShapeDtypeStruct((feat, rows), BF16),
-        in_specs=[vmem, hbm, hbm, hbm, hbm],
+        in_specs=[hbm] * 5,
         out_specs=vmem,
         scratch_shapes=[
+            pltpu.VMEM((1, rows), jnp.int32),
             pltpu.VMEM((rows, width), BF16),
             pltpu.VMEM(w_key.shape, BF16),
             pltpu.VMEM((ny, 2, rk, width + feat), BF16),
@@ -331,21 +334,21 @@
             pltpu.VMEM((total, width), BF16),
             pltpu.VMEM((total, width), BF16),
             pltpu.VMEM((nz, rows, feat), F32),
-            pltpu.VMEM((2, hz, rows, feat), BF16),
-            pltpu.VMEM((2, hz, rows, feat), BF16),
+            pltpu.VMEM((7, rows, feat), BF16),
+            pltpu.VMEM((7, rows, feat), BF16),
             pltpu.VMEM(tiles, BF16),
             pltpu.VMEM((nz, *tiles), BF16),
             pltpu.VMEM(tiles, F32),
             pltpu.VMEM((ny, nq, 2 * CAP, feat), F32),
             pltpu.VMEM((total, feat), BF16),
             pltpu.VMEM((total, feat), BF16),
-            dma((4,)),
+            dma((5,)),
             dma((ny - 1, 2)),
             dma((ny - 1, 2)),
             dma((len(back), nq)),
             dma((len(back), nq)),
-            dma((2, hz)),
-            dma((2, hz)),
+            dma((7,)),
+            dma((7,)),
             dma((len(over_z), nz)),
             dma((len(over_z), nz)),
             dma((len(back), nq)),

time: 61.4 us -> 54.4 us (0.89)
  Pallas kernels: 59.7 us -> 52.7 us
    pallas_call x1, Pallas kernels: 59.7 us -> 52.7 us  [local(): pl.pallas_call(functools.partial(kernel, dims), out_shape=jax.ShapeDtypeS...]
where the time goes in v4:
time: 54.4 us; the launch traced here: 54.2 us
  Pallas kernels  52.7 us (97%)
  local copies, waits for them, and re-layouts  1.54 us (3%)
    pallas_call x1, Pallas kernels, local(): pl.pallas_call(functools.partial(kernel, dims), out_shape=jax.ShapeDtypeS...  52.7 us
    unnamed x1, local copies, waits for them, and re-layouts  1.54 us

profile of v4, /device:TPU:1, one launch (start us, length us, event | category | flops | bytes accessed | tf_op | source)
XLA Modules:
  0.0 54.2 jit_solution(359754219873624783)
XLA Ops:
  0.0 52.7 %shard_map.55 = bf16[128,384]{1,0:T(8,128)(2,1)} custom-call(s32[1,384]{1,0:T(1,128)} %bitcast.3, bf16[384,1024]{1,0:T(8,128)(2,1)} %tok_hbm.1, bf16[1024,1024]{1,0:T(8,128)(2,1)} %w_hbm.1, bf16[2,64,1024]{2,1,0:T(8,128)(2,1)} %bitcast.2, bf16[2,64,1024]{2,1,0:T(8,128)(2,1)} %up_hbm.1), custom_call_target="tpu_custom_call" | custom-call | tf_op jit(solution)/shard_map/pallas_call | solution.py:323
  52.7 1.5 %copy.7 = bf16[128,384]{1,0:T(8,128)(2,1)} copy(bf16[128,384]{1,0:T(8,128)(2,1)} %shard_map.55) | data formatting | bytes 196608

commit v5 on v4

--- a/solution.py
+++ b/solution.py
@@ -14,15 +14,15 @@
 
 def batches(ny):
     half = ny // 2
-    over_z = [[d, ny - d] for d in range(1, half - 1)] + [[0, half - 1, half + 1], [half]]
+    over_z = [[e for d in range(1, half - 1) for e in (d, ny - d)], [0], [half - 1, half + 1], [half]]
     early = [e for d in range(1, half - 1) for e in (d, ny - d)]
     back = ([early] if early else []) + [[half - 1, half + 1], [0, half]]
     return over_z, back
 
 
 def kernel(dims, ids_hbm, tok_hbm, w_hbm, pa_hbm, up_hbm, out_ref,
-           ids_ref, tok, w, panels, place, send, recv, part, zs, zr, rsend, rrecv, rown, widened, lsend, lrecv,
-           in_sem, y_ss, y_rs, x_ss, x_rs, z_ss, z_rs, r_ss, r_rs, l_ss, l_rs):
+           ids_ref, tok, w, panels, ups, place, send, recv, part, zs, zr, rsend, rrecv, rown, srecv, full, widened, lsend, lrecv,
+           in_sem, y_ss, y_rs, u_ss, u_rs, x_ss, x_rs, z_ss, z_rs, r_ss, r_rs, s_ss, s_rs, a_ss, a_rs, l_ss, l_rs):
     nx, ny, nz = dims
     nq = 2 * nx
     half = ny // 2
@@ -55,13 +55,13 @@
         return pltpu.make_async_remote_copy(src, dst, ss, rs, device_id=where, device_id_type=MESH)
 
     barrier = pltpu.get_barrier_semaphore()
-    for step in (-1, 1):
+    for step in (-1, 1, ny // 2):
         pl.semaphore_signal(barrier, inc=1, device_id=along_y(step), device_id_type=MESH)
 
     mine = pl.ds(pl.multiple_of(t * feat, feat), feat)
     loads = [
-        pltpu.make_async_copy(pa_hbm, panels.at[0, :, :, pl.ds(0, width)], in_sem.at[0]),
-        pltpu.make_async_copy(up_hbm.at[:, :, mine], panels.at[0, :, :, pl.ds(width, feat)], in_sem.at[1]),
+        pltpu.make_async_copy(pa_hbm, panels.at[0], in_sem.at[0]),
+        pltpu.make_async_copy(up_hbm.at[:, :, mine], ups.at[0], in_sem.at[1]),
         pltpu.make_async_copy(tok_hbm, tok, in_sem.at[2]),
         pltpu.make_async_copy(ids_hbm, ids_ref, in_sem.at[4]),
         pltpu.make_async_copy(w_hbm, w, in_sem.at[3]),
@@ -77,7 +77,7 @@
     def _(j):
         pl.semaphore_signal(barrier, inc=1, device_id=along_z(lax.rem(t + j, nz)), device_id_type=MESH)
 
-    pl.semaphore_wait(barrier, nq + nz)
+    pl.semaphore_wait(barrier, nq + nz + 1)
 
     below = [(d, j) for d in range(1, half) for j in (0, 1)] + [(half, 0)]
     above = [(d, 1 - j) for d, j in below]
@@ -95,11 +95,25 @@
             if n + 2 < steps:
                 y_copy(n + 2, way).start()
 
+    def u_copy(d, way):
+        src, dst = (-(d - 1) * way) % ny, (-d * way) % ny
+        return remote(ups.at[src], ups.at[dst], u_ss.at[d, (1 - way) // 2], u_rs.at[d, (1 - way) // 2], along_y(way))
+
+    def u_across():
+        return remote(ups.at[0], ups.at[half], u_ss.at[half, 0], u_rs.at[half, 0], along_y(half))
+
+    def u_step(d):
+        for way in (1, -1):
+            if d > 0:
+                u_copy(d, way).wait_recv()
+            if d < half - 1:
+                u_copy(d + 1, way).start()
+
     loads[0].wait()
-    loads[1].wait()
     for n in (0, 1):
         y_copy(n, 1).start()
         y_copy(n, -1).start()
+    loads[1].wait()
 
     loads[3].wait()
     ids = ids_ref[...]
@@ -131,7 +145,7 @@
     def x_copy(b, q, at_q):
         return remote(send.at[block(b, q)], recv.at[block(b, at_q)], x_ss.at[b, q], x_rs.at[b, at_q], along_x(q))
 
-    for b in range(len(back)):
+    for b in (0, 2, 1):
         @pl.loop(1, nq)
         def _(j):
             x_copy(b, lax.rem(mq + j, nq), mq).start()
@@ -187,7 +201,7 @@
         span = len(back[b]) * slots
         x = recv[begin[b]:begin[b] + nq * span, :].reshape(nq, span, width)[:, lo:lo + 2 * slots]
         x = x.reshape(nq * 2 * slots, width)
-        down = jnp.concatenate([panels[e, j, :, :width] for e in offs for j in (0, 1)], axis=0)
+        down = jnp.concatenate([panels[e, j] for e in offs for j in (0, 1)], axis=0)
         r = lax.dot_general(x, down, (((1,), (1,)), ((), ())), preferred_element_type=F32)
         r = r.reshape(nq, 2 * slots, len(offs) * 2 * rk)
         for n, e in enumerate(offs):
@@ -206,16 +220,45 @@
         return remote(rsend.at[these(b)], rrecv.at[at_p, these(b)], r_ss.at[b, p], r_rs.at[b, at_p], along_z(p))
 
     def rank_send(b):
-        pairs = [over_z[b][:1], over_z[b][1:]] if len(over_z[b]) % 2 else [over_z[b]]
-        for offs in pairs:
-            if offs:
-                rank_part(offs)
-
         @pl.loop(1, nz)
         def _(j):
             rank_copy(b, lax.rem(t + j, nz), t).start()
 
         rrecv[t, these(b)] = jnp.zeros((len(over_z[b]), nx * slots, 2 * rk), BF16)
+
+    share = len(over_z[0]) * nx * slots // nz
+    shares = nx * slots // share
+
+    def rows_of(p):
+        return lax.div(p, shares), pl.ds(pl.multiple_of(lax.rem(p, shares) * share, share), share)
+
+    def sum_copy(p, at_p):
+        return remote(rsend.at[rows_of(p)], srecv.at[at_p], s_ss.at[p], s_rs.at[at_p], along_z(p))
+
+    def full_copy(p, at_p):
+        return remote(full.at[at_p], full.at[at_p], a_ss.at[p], a_rs.at[at_p], along_z(p))
+
+    def sum_send():
+        @pl.loop(1, nz)
+        def _(j):
+            sum_copy(lax.rem(t + j, nz), t).start()
+
+        srecv[t] = jnp.zeros((share, 2 * rk), BF16)
+
+    def full_send():
+        @pl.loop(1, nz)
+        def _(j):
+            p = lax.rem(t + j, nz)
+            sum_copy(p, p).wait_recv()
+
+        v = rown[rows_of(t)]
+        for p in range(nz):
+            v = v + srecv[p].astype(F32)
+        full[t] = v
+
+        @pl.loop(1, nz)
+        def _(j):
+            full_copy(lax.rem(t + j, nz), t).start()
 
     def lora_copy(b, q, at_q):
         return remote(lsend.at[block(b, q)], lrecv.at[block(b, at_q)], l_ss.at[b, q], l_rs.at[b, at_q], along_x(q))
@@ -224,13 +267,16 @@
         @pl.loop(1, nz)
         def _(j):
             p = lax.rem(t + j, nz)
-            rank_copy(b, p, p).wait_recv()
+            (rank_copy(b, p, p) if b else full_copy(p, p)).wait_recv()
 
         for e in over_z[b]:
             n = order.index(e)
-            v = rown[n]
-            for p in range(nz):
-                v = v + rrecv[p, n].astype(F32)
+            if b == 0:
+                v = full[n * shares:(n + 1) * shares]
+            else:
+                v = rown[n]
+                for p in range(nz):
+                    v = v + rrecv[p, n].astype(F32)
             v = v.reshape(nx, slots, 2 * rk)
             zero = jnp.zeros_like(v)
             other = swap(v)
@@ -239,8 +285,8 @@
             lhs = jnp.concatenate([even[:, None], odd[:, None]], axis=1).reshape(nq * slots, 2 * rk)
             high = lhs.astype(BF16)
             low = (lhs - high.astype(F32)).astype(BF16)
-            ups = jnp.concatenate([panels[e, j, :, width:] for j in (0, 1)] * 2, axis=0)
-            g = jnp.dot(jnp.concatenate([high, low], axis=1), ups, preferred_element_type=F32)
+            both = jnp.concatenate([ups[e, j] for j in (0, 1)] * 2, axis=0)
+            g = jnp.dot(jnp.concatenate([high, low], axis=1), both, preferred_element_type=F32)
             widened[e] = g.reshape(nq, slots, feat)
         done = [e for o in over_z[:b + 1] for e in o]
         for k, offs in enumerate(back):
@@ -265,28 +311,48 @@
                                preferred_element_type=F32)
 
     last = len(over_z) - 1
-    waited = -1
+    u_at = {2: 0, 4: 1, 6: 2}
     for n in range(steps):
         y_step(n)
+        if n in u_at:
+            u_step(u_at[n])
+        if n == 5:
+            u_across().start()
         if n == 0:
             base_parts()
             z_first()
         if n == steps // 2:
             z_second()
-        b = {2: 0, 3: 1, 5: 2, 6: 3}.get(n) if steps == 7 else {1: 0, 2: 1}.get(n)
-        if b is not None:
-            need = max(where_back[e][0] for e in over_z[b])
-            while waited < need:
-                waited += 1
-                x_wait(waited)
-            rank_send(b)
+        if n == 2:
+            x_wait(0)
+            rank_part(over_z[0][:2])
+        if n == 3:
+            rank_part(over_z[0][2:])
+            sum_send()
+        if n == 4:
+            x_wait(2)
+            rank_part(over_z[1])
+            rank_send(1)
+        if n == 5:
+            x_wait(1)
+            rank_part(over_z[2])
+            rank_send(2)
+            full_send()
+        if n == 6:
+            rank_part(over_z[3])
+            rank_send(3)
     acc = part[t]
     for n in (3, 4, 5, 6):
         z_copy(n).wait_recv()
         acc = acc + zr[n].astype(F32)
     acc = acc.T
-    for b in range(last + 1):
+    for b in range(last):
+        if b == last - 1:
+            for d in range(max(u_at.values()) + 1, half):
+                u_step(d)
         widen(b)
+    u_across().wait_recv()
+    widen(last)
     for b in range(len(back)):
         acc = acc + lora_add(b)
     out_ref[...] = acc.astype(BF16)
@@ -294,6 +360,10 @@
     for n in range(steps):
         y_copy(n, 1).wait_send()
         y_copy(n, -1).wait_send()
+    for d in range(1, half):
+        u_copy(d, 1).wait_send()
+        u_copy(d, -1).wait_send()
+    u_across().wait_send()
     for n in range(7):
         z_copy(n).wait_send()
     for b in range(len(back)):
@@ -302,10 +372,16 @@
             q = lax.rem(mq + j, nq)
             x_copy(b, q, mq).wait_send()
             lora_copy(b, q, mq).wait_send()
-    for b in range(len(over_z)):
+    for b in range(1, len(over_z)):
         @pl.loop(1, nz)
         def _(j):
             rank_copy(b, lax.rem(t + j, nz), t).wait_send()
+
+    @pl.loop(1, nz)
+    def _(j):
+        p = lax.rem(t + j, nz)
+        sum_copy(p, t).wait_send()
+        full_copy(p, t).wait_send()
 
 
 def local(dims, tokens, w_key, row_adapter, panel_a, up_panels):
@@ -320,6 +396,7 @@
     hbm = pl.BlockSpec(memory_space=pl.ANY)
     dma = pltpu.SemaphoreType.DMA
     tiles = (ny, nx * 2 * CAP, 2 * rk)
+    share = len(over_z[0]) * nx * 2 * CAP // nz
     return pl.pallas_call(
         functools.partial(kernel, dims),
         out_shape=jax.ShapeDtypeStruct((feat, rows), BF16),
@@ -329,7 +406,8 @@
             pltpu.VMEM((1, rows), jnp.int32),
             pltpu.VMEM((rows, width), BF16),
             pltpu.VMEM(w_key.shape, BF16),
-            pltpu.VMEM((ny, 2, rk, width + feat), BF16),
+            pltpu.VMEM((ny, 2, rk, width), BF16),
+            pltpu.VMEM((ny, 2, rk, feat), BF16),
             pltpu.VMEM((total, rows), BF16),
             pltpu.VMEM((total, width), BF16),
             pltpu.VMEM((total, width), BF16),
@@ -339,18 +417,26 @@
             pltpu.VMEM(tiles, BF16),
             pltpu.VMEM((nz, *tiles), BF16),
             pltpu.VMEM(tiles, F32),
+            pltpu.VMEM((nz, share, 2 * rk), BF16),
+            pltpu.VMEM((nz, share, 2 * rk), F32),
             pltpu.VMEM((ny, nq, 2 * CAP, feat), F32),
             pltpu.VMEM((total, feat), BF16),
             pltpu.VMEM((total, feat), BF16),
             dma((5,)),
             dma((ny - 1, 2)),
             dma((ny - 1, 2)),
+            dma((ny // 2 + 1, 2)),
+            dma((ny // 2 + 1, 2)),
             dma((len(back), nq)),
             dma((len(back), nq)),
             dma((7,)),
             dma((7,)),
             dma((len(over_z), nz)),
             dma((len(over_z), nz)),
+            dma((nz,)),
+            dma((nz,)),
+            dma((nz,)),
+            dma((nz,)),
             dma((len(back), nq)),
             dma((len(back), nq)),
         ],

time: 54.4 us -> 53 us (0.974)
  Pallas kernels: 52.7 us -> 51.3 us
    pallas_call x1, Pallas kernels: 52.7 us -> 51.3 us  [local(): pl.pallas_call(functools.partial(kernel, dims), out_shape=jax.ShapeDtypeS...]
where the time goes in v5:
time: 53 us; the launch traced here: 52.9 us
  Pallas kernels  51.3 us (97%)
  local copies, waits for them, and re-layouts  1.54 us (3%)
    pallas_call x1, Pallas kernels, local(): pl.pallas_call(functools.partial(kernel, dims), out_shape=jax.ShapeDtypeS...  51.3 us
    unnamed x1, local copies, waits for them, and re-layouts  1.54 us

profile of v5, /device:TPU:1, one launch (start us, length us, event | category | flops | bytes accessed | tf_op | source)
XLA Modules:
  0.0 52.9 jit_solution(10860426442771496486)
XLA Ops:
  0.0 51.3 %shard_map.55 = bf16[128,384]{1,0:T(8,128)(2,1)} custom-call(s32[1,384]{1,0:T(1,128)} %bitcast.3, bf16[384,1024]{1,0:T(8,128)(2,1)} %tok_hbm.1, bf16[1024,1024]{1,0:T(8,128)(2,1)} %w_hbm.1, bf16[2,64,1024]{2,1,0:T(8,128)(2,1)} %bitcast.2, bf16[2,64,1024]{2,1,0:T(8,128)(2,1)} %up_hbm.1), custom_call_target="tpu_custom_call" | custom-call | tf_op jit(solution)/shard_map/pallas_call | solution.py:400
  51.3 1.5 %copy.7 = bf16[128,384]{1,0:T(8,128)(2,1)} copy(bf16[128,384]{1,0:T(8,128)(2,1)} %shard_map.55) | data formatting | bytes 196608

commit v6 on v5

--- a/solution.py
+++ b/solution.py
@@ -334,10 +334,10 @@
             rank_part(over_z[1])
             rank_send(1)
         if n == 5:
+            full_send()
             x_wait(1)
             rank_part(over_z[2])
             rank_send(2)
-            full_send()
         if n == 6:
             rank_part(over_z[3])
             rank_send(3)

time: 53 us -> 52.9 us (level)
  no operation moved by 1% of the time
where the time goes in v6:
time: 52.9 us; the launch traced here: 52.7 us
  Pallas kernels  51.2 us (97%)
  local copies, waits for them, and re-layouts  1.54 us (3%)
    pallas_call x1, Pallas kernels, local(): pl.pallas_call(functools.partial(kernel, dims), out_shape=jax.ShapeDtypeS...  51.2 us
    unnamed x1, local copies, waits for them, and re-layouts  1.54 us

profile of v6, /device:TPU:1, one launch (start us, length us, event | category | flops | bytes accessed | tf_op | source)
XLA Modules:
  0.0 52.7 jit_solution(14423117259893363170)
XLA Ops:
  0.0 51.2 %shard_map.55 = bf16[128,384]{1,0:T(8,128)(2,1)} custom-call(s32[1,384]{1,0:T(1,128)} %bitcast.3, bf16[384,1024]{1,0:T(8,128)(2,1)} %tok_hbm.1, bf16[1024,1024]{1,0:T(8,128)(2,1)} %w_hbm.1, bf16[2,64,1024]{2,1,0:T(8,128)(2,1)} %bitcast.2, bf16[2,64,1024]{2,1,0:T(8,128)(2,1)} %up_hbm.1), custom_call_target="tpu_custom_call" | custom-call | tf_op jit(solution)/shard_map/pallas_call | solution.py:400
  51.2 1.5 %copy.7 = bf16[128,384]{1,0:T(8,128)(2,1)} copy(bf16[128,384]{1,0:T(8,128)(2,1)} %shard_map.55) | data formatting | bytes 196608
